TPU v7x, 128 devices: a whole 4x4x4 slice. The times are simulated.
128 devices in a mesh: row: 8 (over y, core), col: 16 (over z, x).
Axes of the slice: x: 4, y: 4, z: 4, core: 2. Of those that a mesh axis runs over, the one named last changes fastest.
Arguments:
- block_x: float32 [64, 98304], P(None, ('row', 'col')), may hold values from -6 to 6
- block_p: float32 [64, 98304], P(None, ('row', 'col')), may hold values from -6 to 6
- tile_rows: int32 [8, 16, 576], P('row', 'col'), may hold values from 0 to 95, as said below
- tile_cols: int32 [8, 16, 576], P('row', 'col'), may hold values from 0 to 47, as said below
- tile_count: int32 [8, 16], P('row', 'col'), may hold values from 1 to 576, as said below
- tile_vals: bfloat16 [8, 16, 576, 128, 128], P('row', 'col'), may hold values from -0.125 to 0.125
Outputs:
- residual: float32 [64, 98304], P(None, ('row', 'col'))
- image_r: float32 [64, 98304], P(None, ('row', 'col'))
- gram_a: float32 [192, 192], replicated
- gram_b: float32 [192, 192], replicated
Inputs may be any that keep to these rules, and one draw needn't show every extreme that they name: `tile_rows`: within one grid cell the live slots name distinct tiles, all with i <= j; slots at and beyond the cell's count are ignored. `tile_cols`: paired with tile_rows slot by slot. `tile_count`: some grid cell is full in every draw.
All inputs are finite; a program needn't handle non-finite values.
Results may differ from a plain program's by a relative error of at most 0.0035.
Values may be sent and summed in bfloat16 or wider, within the bound.
A program may use at most 128 MiB of HBM per device.

v0:
```python
import math
import jax
import jax.numpy as jnp
from jax import lax
from jax.sharding import PartitionSpec as P


def apply_graph(vectors, tile_rows, tile_cols, live_count, tile_vals):
    vec_width = vectors.shape[0]
    tile_size = tile_vals.shape[-1]
    row_range = lax.all_gather(vectors, "col", axis=1, tiled=True)
    col_group = lax.all_gather(vectors, "row", axis=1, tiled=True)
    row_blocks = row_range.reshape(vec_width, -1, tile_size)
    col_blocks = col_group.reshape(vec_width, -1, tile_size)
    group_size = math.gcd(tile_vals.shape[0], 64)
    offsets = jnp.arange(group_size, dtype=jnp.int32)
    turn_count = (live_count + group_size - 1) // group_size

    def slot_group(turn_index):
        first_slot = turn_index * group_size
        row_index = lax.dynamic_slice_in_dim(tile_rows, first_slot, group_size)
        col_index = lax.dynamic_slice_in_dim(tile_cols, first_slot, group_size)
        values = lax.dynamic_slice_in_dim(tile_vals, first_slot, group_size, 0)
        live_slots = first_slot + offsets < live_count
        return (row_index, col_index, values, live_slots)

    def turn(turn_index, totals):
        row_totals, col_totals = totals
        row_index, col_index, values, live_slots = slot_group(turn_index)
        values = jnp.where(live_slots[:, None, None], values, jnp.zeros_like(values))
        col_inputs = jnp.take(col_blocks, col_index, axis=1)
        row_inputs = jnp.take(row_blocks, row_index, axis=1)
        forward = jnp.einsum("wgb,gab->wga", col_inputs, values, preferred_element_type=jnp.float32)
        backward = jnp.einsum(
            "wga,gab->wgb", row_inputs, values, preferred_element_type=jnp.float32
        )
        return (row_totals.at[:, row_index].add(forward), col_totals.at[:, col_index].add(backward))

    start_rows = jnp.zeros(row_blocks.shape, jnp.float32)
    start_cols = jnp.zeros(col_blocks.shape, jnp.float32)
    row_totals, col_totals = lax.fori_loop(0, turn_count, turn, (start_rows, start_cols))
    own_rows = lax.psum_scatter(
        row_totals.reshape(vec_width, -1), "col", scatter_dimension=1, tiled=True
    )
    own_cols = lax.psum_scatter(
        col_totals.reshape(vec_width, -1), "row", scatter_dimension=1, tiled=True
    )
    return own_rows + own_cols


def per_device(block_x, block_p, tile_rows, tile_cols, tile_count, tile_vals):
    highest = lax.Precision.HIGHEST
    width_k = block_x.shape[0]
    node_count = block_x.shape[1] * lax.axis_size("row") * lax.axis_size("col")
    slot_rows = tile_rows[0, 0]
    slot_cols = tile_cols[0, 0]
    live_count = tile_count[0, 0]
    slot_vals = tile_vals[0, 0]

    def product(left, right):
        return (
            jnp.dot(left, right.T, precision=highest, preferred_element_type=jnp.float32)
            / node_count
        )

    gram_x = lax.psum(product(block_x, block_x), ("row", "col"))
    cholesky_factor = jnp.linalg.cholesky(gram_x)
    orthonormal = lax.linalg.triangular_solve(cholesky_factor, block_x, left_side=True, lower=True)
    ortho_low = orthonormal.astype(jnp.bfloat16)
    dir_low = block_p.astype(jnp.bfloat16)
    both_images = apply_graph(
        jnp.concatenate([ortho_low, dir_low], axis=0), slot_rows, slot_cols, live_count, slot_vals
    )
    image_x = both_images[:width_k]
    image_p = both_images[width_k:]
    rayleigh = lax.psum(product(orthonormal, image_x), ("row", "col"))
    residual = image_x - jnp.dot(
        rayleigh.T, orthonormal, precision=highest, preferred_element_type=jnp.float32
    )
    residual_low = residual.astype(jnp.bfloat16)
    image_r = apply_graph(residual_low, slot_rows, slot_cols, live_count, slot_vals)
    basis = jnp.concatenate([orthonormal, residual, block_p], axis=0)
    images = jnp.concatenate([image_x, image_r, image_p], axis=0)
    gram_a, gram_b = lax.psum((product(basis, images), product(basis, basis)), ("row", "col"))
    return (residual, image_r, gram_a, gram_b)


def solution(mesh):
    in_specs = (
        P(None, ("row", "col")),
        P(None, ("row", "col")),
        P("row", "col", None),
        P("row", "col", None),
        P("row", "col"),
        P("row", "col", None, None, None),
    )
    out_specs = (P(None, ("row", "col")), P(None, ("row", "col")), P(), P())
    return jax.shard_map(
        per_device, mesh=mesh, in_specs=in_specs, out_specs=out_specs, check_vma=False
    )
```

profile of v0, /device:TPU:1, one launch (start us, length us, event | category | flops | bytes accessed | tf_op | source)
XLA Modules:
  0.0 1301.9 jit_solution(9293041823528149920)
XLA Ops:
  8.4 68.9 %psum.28 = f32[64,64]{0,1:T(8,128)S(1)} all-reduce(f32[64,64]{0,1:T(8,128)S(1)} %convolution_multiply_fusion.3), channel_id=1, replica_groups=mesh['row'=8,'col'=16] {'row','col'}, use_global_device_ids=true, to_apply=%region_0.0 | all-reduce | flops 4096 | bytes 32768 | tf_op jit(solution)/shard_map/psum | solution.py:66
  93.1 19.8 %all-gather.4.cloned.1.call-done = bf16[128,6144]{1,0:T(8,128)(2,1)} async-done(((bf16[128,768]{1,0:T(8,128)(2,1)}), bf16[128,6144]{1,0:T(8,128)(2,1)}) %all-gather.4.cloned.1.call-update) | async-done | bytes 1572880 | tf_op jit(solution)/shard_map/all_gather | solution.py:12
  115.9 47.5 %all-gather.6.cloned.1.call-done = bf16[128,12288]{1,0:T(8,128)(2,1)} async-done(((bf16[128,768]{1,0:T(8,128)(2,1)}), bf16[128,12288]{1,0:T(8,128)(2,1)}) %all-gather.6.cloned.1.call-update) | async-done | bytes 3145744 | tf_op jit(solution)/shard_map/all_gather | solution.py:11
  171.6 290.6 %while.26 = (s32[]{:T(128)}, f32[128,96,128]{2,0,1:T(8,128)}, f32[128,48,128]{2,0,1:T(8,128)S(1)}, s32[]{:T(128)}, s32[576]{0:T(1024)S(1)}, /*index=5*/s32[]{:T(...) while((s32[]{:T(128)}, f32[128,96,128]{2,0,1:T(8,128)}, ...), condition=%wide.region_6.7_spmd.clone, body=%wide.region_3.6_spmd.clone.sunk | while | flops 543165312 | bytes 50343056 | solution.py:41
  181.7 13.6 %scatter_fusion = f32[128,96,128]{2,0,1:T(8,128)} fusion(f32[128,96,128]{2,0,1:T(8,128)} %get-tuple-element.407, s32[64]{0:T(128)S(1)} %get-tuple-element.374, f32[64,128,128]{2,1,0:T(8,128)} %fusion.80), kind=kCustom, calls=%fused_computation.4.clone.clone.1 | custom fusion | flops 1048576 | bytes 12583168 | tf_op jit(solution)/shard_map/while/body/scatter-add | solution.py:37
  223.2 13.6 %scatter_fusion = f32[128,96,128]{2,0,1:T(8,128)} fusion(f32[128,96,128]{2,0,1:T(8,128)} %get-tuple-element.407, s32[64]{0:T(128)S(1)} %get-tuple-element.374, f32[64,128,128]{2,1,0:T(8,128)} %fusion.80), kind=kCustom, calls=%fused_computation.4.clone.clone.1 | custom fusion | flops 1048576 | bytes 12583168 | tf_op jit(solution)/shard_map/while/body/scatter-add | solution.py:37
  264.8 13.6 %scatter_fusion = f32[128,96,128]{2,0,1:T(8,128)} fusion(f32[128,96,128]{2,0,1:T(8,128)} %get-tuple-element.407, s32[64]{0:T(128)S(1)} %get-tuple-element.374, f32[64,128,128]{2,1,0:T(8,128)} %fusion.80), kind=kCustom, calls=%fused_computation.4.clone.clone.1 | custom fusion | flops 1048576 | bytes 12583168 | tf_op jit(solution)/shard_map/while/body/scatter-add | solution.py:37
  306.3 13.5 %scatter_fusion = f32[128,96,128]{2,0,1:T(8,128)} fusion(f32[128,96,128]{2,0,1:T(8,128)} %get-tuple-element.407, s32[64]{0:T(128)S(1)} %get-tuple-element.374, f32[64,128,128]{2,1,0:T(8,128)} %fusion.80), kind=kCustom, calls=%fused_computation.4.clone.clone.1 | custom fusion | flops 1048576 | bytes 12583168 | tf_op jit(solution)/shard_map/while/body/scatter-add | solution.py:37
  347.7 13.6 %scatter_fusion = f32[128,96,128]{2,0,1:T(8,128)} fusion(f32[128,96,128]{2,0,1:T(8,128)} %get-tuple-element.407, s32[64]{0:T(128)S(1)} %get-tuple-element.374, f32[64,128,128]{2,1,0:T(8,128)} %fusion.80), kind=kCustom, calls=%fused_computation.4.clone.clone.1 | custom fusion | flops 1048576 | bytes 12583168 | tf_op jit(solution)/shard_map/while/body/scatter-add | solution.py:37
  389.2 13.6 %scatter_fusion = f32[128,96,128]{2,0,1:T(8,128)} fusion(f32[128,96,128]{2,0,1:T(8,128)} %get-tuple-element.407, s32[64]{0:T(128)S(1)} %get-tuple-element.374, f32[64,128,128]{2,1,0:T(8,128)} %fusion.80), kind=kCustom, calls=%fused_computation.4.clone.clone.1 | custom fusion | flops 1048576 | bytes 12583168 | tf_op jit(solution)/shard_map/while/body/scatter-add | solution.py:37
  430.7 13.6 %scatter_fusion = f32[128,96,128]{2,0,1:T(8,128)} fusion(f32[128,96,128]{2,0,1:T(8,128)} %get-tuple-element.407, s32[64]{0:T(128)S(1)} %get-tuple-element.374, f32[64,128,128]{2,1,0:T(8,128)} %fusion.80), kind=kCustom, calls=%fused_computation.4.clone.clone.1 | custom fusion | flops 1048576 | bytes 12583168 | tf_op jit(solution)/shard_map/while/body/scatter-add | solution.py:37
  470.4 106.4 %reduce-scatter.7.cloned.1.call-done = f32[128,768]{1,0:T(8,128)} async-done(((f32[128,6144]{1,0:T(8,128)}), f32[128,768]{1,0:T(8,128)}) %reduce-scatter.7.cloned.1.call-update) | async-done | bytes 393232 | tf_op jit(solution)/shard_map/reduce_scatter | solution.py:45
  576.8 85.4 %reduce-scatter.5.cloned.1.call-done = f32[128,768]{1,0:T(8,128)} async-done(((f32[128,12288]{1,0:T(8,128)}), f32[128,768]{1,0:T(8,128)}) %reduce-scatter.5.cloned.1.call-update) | async-done | bytes 393232 | tf_op jit(solution)/shard_map/reduce_scatter | solution.py:42
  663.6 65.7 %psum.29 = f32[64,64]{0,1:T(8,128)S(1)} all-reduce(f32[64,64]{0,1:T(8,128)S(1)} %convolution_multiply_fusion.2), channel_id=1, replica_groups=mesh['row'=8,'col'=16] {'row','col'}, use_global_device_ids=true, to_apply=%region_9.10 | all-reduce | flops 4096 | bytes 32768 | tf_op jit(solution)/shard_map/psum | solution.py:76
  730.4 14.3 %all_gather.14 = bf16[64,6144]{1,0:T(8,128)(2,1)S(1)} all-gather(bf16[64,768]{1,0:T(8,128)(2,1)} %get-tuple-element.250), channel_id=1, replica_groups=mesh['row'=8,'col'=16] {'row'}, dimensions={1}, use_global_device_ids=true | all-gather | bytes 884736 | tf_op jit(solution)/shard_map/all_gather | solution.py:12
  745.8 24.0 %all-gather.8.cloned.1.call-done = bf16[64,12288]{1,0:T(8,128)(2,1)} async-done(((bf16[64,768]{1,0:T(8,128)(2,1)}), bf16[64,12288]{1,0:T(8,128)(2,1)}) %all-gather.8.cloned.1.call-update) | async-done | bytes 1572880 | tf_op jit(solution)/shard_map/all_gather | solution.py:11
  776.2 198.4 %while.27 = (s32[]{:T(128)}, f32[64,96,128]{2,0,1:T(8,128)}, f32[64,48,128]{2,0,1:T(8,128)}, s32[]{:T(128)}, s32[576]{0:T(1024)S(1)}, /*index=5*/s32[]{:T(128)},...) while((s32[]{:T(128)}, f32[64,96,128]{2,0,1:T(8,128)}, ...), condition=%wide.region_13.14_spmd.clone, body=%wide.region_10.13_spmd.clone.sunk | while | flops 272632704 | bytes 27274384 | solution.py:41
  782.0 9.0 scatter_fusion.2
  795.5 9.0 scatter_fusion.3
  838.7 9.0 scatter_fusion.2
  923.6 9.1 scatter_fusion.2
  981.7 80.2 %reduce-scatter.11.cloned.1.call-done = f32[64,768]{1,0:T(8,128)} async-done(((f32[64,6144]{1,0:T(8,128)}), f32[64,768]{1,0:T(8,128)}) %reduce-scatter.11.cloned.1.call-update) | async-done | bytes 196624 | tf_op jit(solution)/shard_map/reduce_scatter | solution.py:45
  1061.9 79.4 %reduce-scatter.9.cloned.1.call-done = f32[64,768]{1,0:T(8,128)} async-done(((f32[64,12288]{1,0:T(8,128)}), f32[64,768]{1,0:T(8,128)}) %reduce-scatter.9.cloned.1.call-update) | async-done | bytes 196624 | tf_op jit(solution)/shard_map/reduce_scatter | solution.py:42
  1143.7 148.1 %all-reduce.3.cloned.1.call-done = (f32[192,192]{1,0:T(8,128)}, f32[192,192]{1,0:T(8,128)}) async-done(((f32[192,192]{1,0:T(8,128)}, f32[192,192]{1,0:T(8,128)}), (f32[192,192]{1,0:T(8,128)}, f32[192,192]{1,0:T(8,128)})) %all-reduce.3.cloned.1.call-update) | async-done | bytes 294928 | tf_op jit(solution)/shard_map/psum | solution.py:84
  (199 shorter events, 415.5 us)
Async XLA Ops:
  7.2 0.9 copy-start
  7.2 85.8 %copy-start.8 = (s32[1,1,576]{2,1,0:T(1,128)S(1)}, s32[1,1,576]{2,1,0:T(1,128)}, u32[]{:S(2)}) copy-start(s32[1,1,576]{2,1,0:T(1,128)} %param.12) | copy-start | bytes 6916
  7.2 85.8 %copy-start.9 = (s32[1,1,576]{2,1,0:T(1,128)S(1)}, s32[1,1,576]{2,1,0:T(1,128)}, u32[]{:S(2)}) copy-start(s32[1,1,576]{2,1,0:T(1,128)} %param.13) | copy-start | bytes 6916
  7.2 105.7 %all-gather.4.cloned.1.call-start = ((), (), s32[]{:S(2)}) async-start(), calls=%async_computation.4 | async-start | bytes 1769472 | tf_op jit(solution)/shard_map/all_gather | solution.py:12
  91.5 71.8 %all-gather.6.cloned.1.call-start = ((), (), s32[]{:S(2)}) async-start(), calls=%async_computation.5 | async-start | bytes 3342336 | tf_op jit(solution)/shard_map/all_gather | solution.py:11
  92.3 484.5 %reduce-scatter.7.cloned.1.call-start = ((), (), s32[]{:S(2)}) async-start(), calls=%async_computation.7 | async-start | bytes 3538944 | tf_op jit(solution)/shard_map/reduce_scatter | solution.py:45
  464.2 198.0 %reduce-scatter.5.cloned.1.call-start = ((), (), s32[]{:S(2)}) async-start(), calls=%async_computation.6 | async-start | bytes 6684672 | tf_op jit(solution)/shard_map/reduce_scatter | solution.py:42
  470.3 299.4 %all-gather.8.cloned.1.call-start = ((), (), s32[]{:S(2)}) async-start(), calls=%async_computation.8 | async-start | bytes 1671168 | tf_op jit(solution)/shard_map/all_gather | solution.py:11
  663.3 109.5 %copy-start.3 = (f32[128,768]{1,0:T(8,128)}, f32[128,768]{1,0:T(8,128)S(1)}, u32[]{:S(2)}) copy-start(f32[128,768]{1,0:T(8,128)S(1)} %add.116) | copy-start | bytes 1179652
  730.3 331.6 %reduce-scatter.11.cloned.1.call-start = ((), (), s32[]{:S(2)}) async-start(), calls=%async_computation.10 | async-start | bytes 1769472 | tf_op jit(solution)/shard_map/reduce_scatter | solution.py:45
  974.6 2.9 copy-start.2
  977.4 163.9 %reduce-scatter.9.cloned.1.call-start = ((), (), s32[]{:S(2)}) async-start(), calls=%async_computation.9 | async-start | bytes 3342336 | tf_op jit(solution)/shard_map/reduce_scatter | solution.py:42
  979.3 0.9 copy-start.5
  979.3 1.0 copy-start.6
  979.3 2.3 copy-start.4
  979.3 312.4 %all-reduce.3.cloned.1.call-start = ((), (), s32[]{:S(2)}) async-start(), calls=%async_computation.11 | async-start | bytes 786432 | tf_op jit(solution)/shard_map/psum | solution.py:84
  980.3 314.7 %copy-start.1 = (f32[64,768]{1,0:T(8,128)S(1)}, f32[64,768]{1,0:T(8,128)}, u32[]{:S(2)}) copy-start(f32[64,768]{1,0:T(8,128)} %param.10) | copy-start | bytes 589828
  1142.3 152.7 %copy-start.7 = (f32[64,768]{1,0:T(8,128)}, f32[64,768]{1,0:T(8,128)S(1)}, u32[]{:S(2)}) copy-start(f32[64,768]{1,0:T(8,128)S(1)} %add.117) | copy-start | bytes 589828
Sparse Core Ops, SparseCore 0:
  91.7 21.1 all-gather.3
  115.6 47.6 all-gather.5
  464.3 112.4 reduce-scatter.6
  580.0 82.0 reduce-scatter.4
  730.4 39.2 all-gather.7
  977.5 84.3 reduce-scatter.10
  1065.2 76.0 reduce-scatter.8
  1146.6 145.1 all-reduce.2
where the time goes:
time: 1310 us; the launch traced here: 1300 us
  waiting for transfers between devices  591 us (45%)
  other arithmetic  309 us (24%)
  blocking collectives  149 us (11%)
  local copies, waits for them, and re-layouts  118 us (9%)
  matrix products  118 us (9%)
  between operations  15 us (1%)
    reduce_scatter x2, waiting for transfers between devices, apply_graph(): lax.psum_scatter(col_totals.reshape(vec_width, -1), 'row', scatter_dimens...  187 us
    reduce_scatter x2, waiting for transfers between devices, apply_graph(): lax.psum_scatter(row_totals.reshape(vec_width, -1), 'col', scatter_dimens...  165 us
    scatter-add x14, other arithmetic, turn(): row_totals.at[:, row_index].add(forward)  158 us
    psum x1, waiting for transfers between devices, per_device(): lax.psum((product(basis, images), product(basis, basis)), ('row', 'col'))  148 us
    scatter-add x14, other arithmetic, turn(): col_totals.at[:, col_index].add(backward)  125 us
    all_gather x2, waiting for transfers between devices, apply_graph(): row_range = lax.all_gather(vectors, 'col', axis=1, tiled=True)  71.4 us
    psum x1, blocking collectives, per_device(): gram_x = lax.psum(product(block_x, block_x), ('row', 'col'))  68.9 us
    psum x1, blocking collectives, per_device(): rayleigh = lax.psum(product(orthonormal, image_x), ('row', 'col'))  65.7 us
  transfers between devices with their start and end apart: 8, of which 8 were waited for; matrix products, arithmetic and copies ran while one was open for 1% of the time, Pallas kernels for 0%

commit v1 on v0

--- a/solution.py
+++ b/solution.py
@@ -8,7 +8,15 @@
 def apply_graph(vectors, tile_rows, tile_cols, live_count, tile_vals):
     vec_width = vectors.shape[0]
     tile_size = tile_vals.shape[-1]
-    row_range = lax.all_gather(vectors, "col", axis=1, tiled=True)
+    ways, here = (lax.axis_size("col"), lax.axis_index("col"))
+    grown, reach = (vectors, 1)
+    while reach < ways:
+        theirs = lax.ppermute(grown, "col", [(d, d ^ reach) for d in range(ways)])
+        mine_first = jnp.concatenate([grown, theirs], axis=1)
+        theirs_first = jnp.concatenate([theirs, grown], axis=1)
+        grown = jnp.where(here & reach == 0, mine_first, theirs_first)
+        reach = 2 * reach
+    row_range = grown
     col_group = lax.all_gather(vectors, "row", axis=1, tiled=True)
     row_blocks = row_range.reshape(vec_width, -1, tile_size)
     col_blocks = col_group.reshape(vec_width, -1, tile_size)

time: 1310 us -> 1320 us (level)
  waiting for transfers between devices: 591 us -> 576 us
    all_gather x2 -> x0, waiting for transfers between devices: 71.4 us -> none  [apply_graph(): row_range = lax.all_gather(vectors, 'col', axis=1, tiled=True)]
    ppermute x0 -> x8, waiting for transfers between devices: none -> 70.7 us  [apply_graph(): theirs = lax.ppermute(grown, 'col', [(d, d ^ reach) for d in range(ways)])]
    all_gather x1, waiting for transfers between devices: 19.8 us -> 2.81 us  [apply_graph(): col_group = lax.all_gather(vectors, 'row', axis=1, tiled=True)]
  transfers between devices with their start and end apart: 8 -> 14, of which waited for: 8 -> 13; matrix products, arithmetic and copies ran while one was open for 1% -> 1% of each run, Pallas kernels for 0% -> 0%
where the time goes in v1:
time: 1320 us; the launch traced here: 1310 us
  waiting for transfers between devices  576 us (44%)
  other arithmetic  319 us (24%)
  blocking collectives  152 us (12%)
  local copies, waits for them, and re-layouts  120 us (9%)
  matrix products  118 us (9%)
  between operations  15.2 us (1%)
    reduce_scatter x2, waiting for transfers between devices, apply_graph(): lax.psum_scatter(col_totals.reshape(vec_width, -1), 'row', scatter_dimens...  189 us
    reduce_scatter x2, waiting for transfers between devices, apply_graph(): lax.psum_scatter(row_totals.reshape(vec_width, -1), 'col', scatter_dimens...  165 us
    scatter-add x14, other arithmetic, turn(): row_totals.at[:, row_index].add(forward)  160 us
    psum x1, waiting for transfers between devices, per_device(): lax.psum((product(basis, images), product(basis, basis)), ('row', 'col'))  148 us
    scatter-add x14, other arithmetic, turn(): col_totals.at[:, col_index].add(backward)  125 us
    ppermute x8, waiting for transfers between devices, apply_graph(): theirs = lax.ppermute(grown, 'col', [(d, d ^ reach) for d in range(ways)])  70.7 us
    psum x1, blocking collectives, per_device(): gram_x = lax.psum(product(block_x, block_x), ('row', 'col'))  68.9 us
    psum x1, blocking collectives, per_device(): rayleigh = lax.psum(product(orthonormal, image_x), ('row', 'col'))  65.5 us
  transfers between devices with their start and end apart: 14, of which 13 were waited for; matrix products, arithmetic and copies ran while one was open for 1% of the time, Pallas kernels for 0%

profile of v1, /device:TPU:1, one launch (start us, length us, event | category | flops | bytes accessed | tf_op | source)
XLA Modules:
  0.0 1306.1 jit_solution(6382954447680194586)
XLA Ops:
  8.4 68.9 %psum.28 = f32[64,64]{0,1:T(8,128)S(1)} all-reduce(f32[64,64]{0,1:T(8,128)S(1)} %convolution_multiply_fusion.3), channel_id=1, replica_groups=mesh['row'=8,'col'=16] {'row','col'}, use_global_device_ids=true, to_apply=%region_0.0 | all-reduce | flops 4096 | bytes 32768 | tf_op jit(solution)/shard_map/psum | solution.py:74
  97.9 9.2 collective-permute-done.1
  107.4 16.2 %collective-permute-done.2 = bf16[128,3072]{1,0:T(8,128)(2,1)S(1)} collective-permute-done((bf16[128,3072]{1,0:T(8,128)(2,1)S(1)}, bf16[128,3072]{1,0:T(8,128)(2,1)S(1)}, u32[]{:S(2)}, u32[]{:S(2)}) %collective-permute-start.2) | collective-permute-done | bytes 786464 | tf_op jit(solution)/shard_map/ppermute | solution.py:14
  135.3 24.0 %collective-permute-done.3 = bf16[128,6144]{1,0:T(8,128)(2,1)} collective-permute-done((bf16[128,6144]{1,0:T(8,128)(2,1)}, bf16[128,6144]{1,0:T(8,128)(2,1)}, u32[]{:S(2)}, u32[]{:S(2)}) %collective-permute-start.3) | collective-permute-done | bytes 1572896 | tf_op jit(solution)/shard_map/ppermute | solution.py:14
  171.7 291.1 %while.26 = (s32[]{:T(128)}, f32[128,96,128]{2,0,1:T(8,128)}, f32[128,48,128]{2,0,1:T(8,128)S(1)}, s32[]{:T(128)}, s32[576]{0:T(1024)S(1)}, /*index=5*/s32[]{:T(...) while((s32[]{:T(128)}, f32[128,96,128]{2,0,1:T(8,128)}, ...), condition=%wide.region_6.7_spmd.clone, body=%wide.region_3.6_spmd.clone.sunk | while | flops 543165312 | bytes 50343056 | solution.py:49
  182.0 13.7 %scatter_fusion = f32[128,96,128]{2,0,1:T(8,128)} fusion(f32[128,96,128]{2,0,1:T(8,128)} %get-tuple-element.407, s32[64]{0:T(128)S(1)} %get-tuple-element.374, f32[64,128,128]{2,1,0:T(8,128)} %fusion.78), kind=kCustom, calls=%fused_computation.4.clone.clone.1 | custom fusion | flops 1048576 | bytes 12583168 | tf_op jit(solution)/shard_map/while/body/scatter-add | solution.py:45
  223.6 13.7 %scatter_fusion = f32[128,96,128]{2,0,1:T(8,128)} fusion(f32[128,96,128]{2,0,1:T(8,128)} %get-tuple-element.407, s32[64]{0:T(128)S(1)} %get-tuple-element.374, f32[64,128,128]{2,1,0:T(8,128)} %fusion.78), kind=kCustom, calls=%fused_computation.4.clone.clone.1 | custom fusion | flops 1048576 | bytes 12583168 | tf_op jit(solution)/shard_map/while/body/scatter-add | solution.py:45
  265.1 13.7 %scatter_fusion = f32[128,96,128]{2,0,1:T(8,128)} fusion(f32[128,96,128]{2,0,1:T(8,128)} %get-tuple-element.407, s32[64]{0:T(128)S(1)} %get-tuple-element.374, f32[64,128,128]{2,1,0:T(8,128)} %fusion.78), kind=kCustom, calls=%fused_computation.4.clone.clone.1 | custom fusion | flops 1048576 | bytes 12583168 | tf_op jit(solution)/shard_map/while/body/scatter-add | solution.py:45
  306.7 13.6 %scatter_fusion = f32[128,96,128]{2,0,1:T(8,128)} fusion(f32[128,96,128]{2,0,1:T(8,128)} %get-tuple-element.407, s32[64]{0:T(128)S(1)} %get-tuple-element.374, f32[64,128,128]{2,1,0:T(8,128)} %fusion.78), kind=kCustom, calls=%fused_computation.4.clone.clone.1 | custom fusion | flops 1048576 | bytes 12583168 | tf_op jit(solution)/shard_map/while/body/scatter-add | solution.py:45
  348.2 13.8 %scatter_fusion = f32[128,96,128]{2,0,1:T(8,128)} fusion(f32[128,96,128]{2,0,1:T(8,128)} %get-tuple-element.407, s32[64]{0:T(128)S(1)} %get-tuple-element.374, f32[64,128,128]{2,1,0:T(8,128)} %fusion.78), kind=kCustom, calls=%fused_computation.4.clone.clone.1 | custom fusion | flops 1048576 | bytes 12583168 | tf_op jit(solution)/shard_map/while/body/scatter-add | solution.py:45
  389.9 13.7 %scatter_fusion = f32[128,96,128]{2,0,1:T(8,128)} fusion(f32[128,96,128]{2,0,1:T(8,128)} %get-tuple-element.407, s32[64]{0:T(128)S(1)} %get-tuple-element.374, f32[64,128,128]{2,1,0:T(8,128)} %fusion.78), kind=kCustom, calls=%fused_computation.4.clone.clone.1 | custom fusion | flops 1048576 | bytes 12583168 | tf_op jit(solution)/shard_map/while/body/scatter-add | solution.py:45
  431.4 13.7 %scatter_fusion = f32[128,96,128]{2,0,1:T(8,128)} fusion(f32[128,96,128]{2,0,1:T(8,128)} %get-tuple-element.407, s32[64]{0:T(128)S(1)} %get-tuple-element.374, f32[64,128,128]{2,1,0:T(8,128)} %fusion.78), kind=kCustom, calls=%fused_computation.4.clone.clone.1 | custom fusion | flops 1048576 | bytes 12583168 | tf_op jit(solution)/shard_map/while/body/scatter-add | solution.py:45
  471.0 110.2 %reduce-scatter.7.cloned.1.call-done = f32[128,768]{1,0:T(8,128)} async-done(((f32[128,6144]{1,0:T(8,128)}), f32[128,768]{1,0:T(8,128)}) %reduce-scatter.7.cloned.1.call-update) | async-done | bytes 393232 | tf_op jit(solution)/shard_map/reduce_scatter | solution.py:53
  581.2 85.7 %reduce-scatter.5.cloned.1.call-done = f32[128,768]{1,0:T(8,128)} async-done(((f32[128,12288]{1,0:T(8,128)}), f32[128,768]{1,0:T(8,128)}) %reduce-scatter.5.cloned.1.call-update) | async-done | bytes 393232 | tf_op jit(solution)/shard_map/reduce_scatter | solution.py:50
  668.4 65.5 %psum.29 = f32[64,64]{0,1:T(8,128)S(1)} all-reduce(f32[64,64]{0,1:T(8,128)S(1)} %convolution_multiply_fusion.2), channel_id=1, replica_groups=mesh['row'=8,'col'=16] {'row','col'}, use_global_device_ids=true, to_apply=%region_9.10 | all-reduce | flops 4096 | bytes 32768 | tf_op jit(solution)/shard_map/psum | solution.py:84
  753.4 17.8 %all_gather.7 = bf16[64,6144]{1,0:T(8,128)(2,1)S(1)} all-gather(bf16[64,768]{1,0:T(8,128)(2,1)S(1)} %get-tuple-element.250), channel_id=1, replica_groups=mesh['row'=8,'col'=16] {'row'}, dimensions={1}, use_global_device_ids=true | all-gather | bytes 884736 | tf_op jit(solution)/shard_map/all_gather | solution.py:20
  780.3 200.0 %while.27 = (s32[]{:T(128)}, f32[64,96,128]{2,0,1:T(8,128)}, f32[64,48,128]{2,0,1:T(8,128)}, s32[]{:T(128)}, s32[576]{0:T(1024)S(1)}, /*index=5*/s32[]{:T(128)},...) while((s32[]{:T(128)}, f32[64,96,128]{2,0,1:T(8,128)}, ...), condition=%wide.region_13.14_spmd.clone, body=%wide.region_10.13_spmd.clone.sunk | while | flops 272632704 | bytes 27274384 | solution.py:49
  799.7 9.1 scatter_fusion.3
  814.7 9.2 scatter_fusion.2
  828.4 9.2 scatter_fusion.3
  857.0 9.2 scatter_fusion.3
  987.4 79.0 %reduce-scatter.11.cloned.1.call-done = f32[64,768]{1,0:T(8,128)} async-done(((f32[64,6144]{1,0:T(8,128)}), f32[64,768]{1,0:T(8,128)}) %reduce-scatter.11.cloned.1.call-update) | async-done | bytes 196624 | tf_op jit(solution)/shard_map/reduce_scatter | solution.py:53
  1066.4 79.1 %reduce-scatter.9.cloned.1.call-done = f32[64,768]{1,0:T(8,128)} async-done(((f32[64,12288]{1,0:T(8,128)}), f32[64,768]{1,0:T(8,128)}) %reduce-scatter.9.cloned.1.call-update) | async-done | bytes 196624 | tf_op jit(solution)/shard_map/reduce_scatter | solution.py:50
  1148.0 148.0 %all-reduce.3.cloned.1.call-done = (f32[192,192]{1,0:T(8,128)}, f32[192,192]{1,0:T(8,128)}) async-done(((f32[192,192]{1,0:T(8,128)}, f32[192,192]{1,0:T(8,128)}), (f32[192,192]{1,0:T(8,128)}, f32[192,192]{1,0:T(8,128)})) %all-reduce.3.cloned.1.call-update) | async-done | bytes 294928 | tf_op jit(solution)/shard_map/psum | solution.py:92
  (237 shorter events, 454.2 us)
Async XLA Ops:
  7.2 125.1 %all-gather.2.cloned.1.call-start = ((), (), s32[]{:S(2)}) async-start(), calls=%async_computation.4 | async-start | bytes 1769472 | tf_op jit(solution)/shard_map/all_gather | solution.py:20
  90.8 16.5 %copy-start.5 = (bf16[128,768]{1,0:T(8,128)(2,1)}, bf16[128,768]{1,0:T(8,128)(2,1)S(1)}, u32[]{:S(2)}) copy-start(bf16[128,768]{1,0:T(8,128)(2,1)S(1)} %pad_maximum_fusion.3) | copy-start | bytes 589828
  90.9 5.6 collective-permute-start
  96.6 10.4 collective-permute-start.1
  107.2 19.8 %copy-start.10 = (s32[1,1,576]{2,1,0:T(1,128)S(1)}, s32[1,1,576]{2,1,0:T(1,128)}, u32[]{:S(2)}) copy-start(s32[1,1,576]{2,1,0:T(1,128)} %param.12) | copy-start | bytes 6916
  107.2 19.9 %copy-start.11 = (s32[1,1,576]{2,1,0:T(1,128)S(1)}, s32[1,1,576]{2,1,0:T(1,128)}, u32[]{:S(2)}) copy-start(s32[1,1,576]{2,1,0:T(1,128)} %param.13) | copy-start | bytes 6916
  107.2 16.4 %collective-permute-start.2 = (bf16[128,3072]{1,0:T(8,128)(2,1)S(1)}, bf16[128,3072]{1,0:T(8,128)(2,1)S(1)}, u32[]{:S(2)}, u32[]{:S(2)}) collective-permute-start(bf16[128,3072]{1,0:T(8,128)(2,1)S(1)} %maximum_select_fusion.5), channel_id=1, source_target_pairs={{0,4},{1,5},{2,6},{3,7},{4,0},{5,1},{6,2},{7,3},{8,12},{9,13},{10,... | collective-permute-start | bytes 2359304 | tf_op jit(solution)/shard_map/ppermute | solution.py:14
  107.4 19.5 %copy-start.6 = (bf16[128,768]{1,0:T(8,128)(2,1)S(1)}, bf16[128,768]{1,0:T(8,128)(2,1)}, u32[]{:S(2)}) copy-start(bf16[128,768]{1,0:T(8,128)(2,1)} %copy-done.5) | copy-start | bytes 589828
  107.4 473.8 %reduce-scatter.7.cloned.1.call-start = ((), (), s32[]{:S(2)}) async-start(), calls=%async_computation.6 | async-start | bytes 3538944 | tf_op jit(solution)/shard_map/reduce_scatter | solution.py:53
  125.2 34.1 %collective-permute-start.3 = (bf16[128,6144]{1,0:T(8,128)(2,1)}, bf16[128,6144]{1,0:T(8,128)(2,1)}, u32[]{:S(2)}, u32[]{:S(2)}) collective-permute-start(bf16[128,6144]{1,0:T(8,128)(2,1)} %maximum_select_fusion.2), channel_id=1, source_target_pairs={{0,8},{1,9},{2,10},{3,11},{4,12},{5,13},{6,14},{7,15},{8,0},{9,1},... | collective-permute-start | bytes 4718600 | tf_op jit(solution)/shard_map/ppermute | solution.py:14
  464.8 202.0 %reduce-scatter.5.cloned.1.call-start = ((), (), s32[]{:S(2)}) async-start(), calls=%async_computation.5 | async-start | bytes 6684672 | tf_op jit(solution)/shard_map/reduce_scatter | solution.py:50
  471.0 595.5 %reduce-scatter.11.cloned.1.call-start = ((), (), s32[]{:S(2)}) async-start(), calls=%async_computation.8 | async-start | bytes 1769472 | tf_op jit(solution)/shard_map/reduce_scatter | solution.py:53
  668.0 103.1 %copy-start.3 = (f32[128,768]{1,0:T(8,128)}, f32[128,768]{1,0:T(8,128)S(1)}, u32[]{:S(2)}) copy-start(f32[128,768]{1,0:T(8,128)S(1)} %add.116) | copy-start | bytes 1179652
  734.8 3.5 collective-permute-start.4
  738.3 6.1 collective-permute-start.5
  744.5 7.5 collective-permute-start.6
  752.2 21.2 %collective-permute-start.7 = (bf16[64,6144]{1,0:T(8,128)(2,1)S(1)}, bf16[64,6144]{1,0:T(8,128)(2,1)}, u32[]{:S(2)}, u32[]{:S(2)}) collective-permute-start(bf16[64,6144]{1,0:T(8,128)(2,1)S(1)} %maximum_select_fusion.7), channel_id=1, source_target_pairs={{0,8},{1,9},{2,10},{3,11},{4,12},{5,13},{6,14},{7,15},{8,0},{9,1},... | collective-permute-start | bytes 2359304 | tf_op jit(solution)/shard_map/ppermute | solution.py:14
  980.3 2.9 copy-start.2
  983.1 162.4 %reduce-scatter.9.cloned.1.call-start = ((), (), s32[]{:S(2)}) async-start(), calls=%async_computation.7 | async-start | bytes 3342336 | tf_op jit(solution)/shard_map/reduce_scatter | solution.py:50
  985.0 1.0 copy-start.8
  985.0 2.3 copy-start.4
  985.1 310.9 %all-reduce.3.cloned.1.call-start = ((), (), s32[]{:S(2)}) async-start(), calls=%async_computation.9 | async-start | bytes 786432 | tf_op jit(solution)/shard_map/psum | solution.py:92
  986.1 313.2 %copy-start.1 = (f32[64,768]{1,0:T(8,128)S(1)}, f32[64,768]{1,0:T(8,128)}, u32[]{:S(2)}) copy-start(f32[64,768]{1,0:T(8,128)} %param.10) | copy-start | bytes 589828
  1146.6 152.6 %copy-start.9 = (f32[64,768]{1,0:T(8,128)}, f32[64,768]{1,0:T(8,128)S(1)}, u32[]{:S(2)}) copy-start(f32[64,768]{1,0:T(8,128)S(1)} %add.117) | copy-start | bytes 589828
  (2 other events, 1.9 us)
Sparse Core Ops, SparseCore 0:
  107.5 24.7 all-gather.1
  465.0 116.2 reduce-scatter.6
  584.7 82.1 reduce-scatter.4
  983.3 83.1 reduce-scatter.10
  1069.6 75.8 reduce-scatter.8
  1150.8 145.1 all-reduce.2
